TPU v7x, 512 devices: a whole 4x8x8 slice. The times are simulated.
512 devices in a mesh: replica: 32 (over z, y_lo, core), fsdp: 16 (over x, y_hi).
Axes of the slice: x: 4, y: 8 (y_hi: 4, y_lo: 2; y = y_hi * 2 + y_lo), z: 8, core: 2. Of those that a mesh axis runs over, the one named last changes fastest.
Arguments:
- features: bfloat16 [65536, 8192], P(('replica', 'fsdp')), may hold values from -6 to 6
- cotangents: bfloat16 [65536, 512], P(('replica', 'fsdp')), may hold values from -0.13183594 to 0.13183594
- params: bfloat16 [32, 512, 8192], P('replica', None, 'fsdp'), may hold values from -6.5 to 6.5
- first_moment: bfloat16 [32, 512, 8192], P('replica', None, 'fsdp'), may hold values from -5 to 5
- second_moment: bfloat16 [32, 512, 8192], P('replica', None, 'fsdp'), may hold values from 0.25 to 4
- anchor: float32 [512, 8192], P('replica', 'fsdp'), may hold values from -5 to 5
- outer_momentum: float32 [512, 8192], P('replica', 'fsdp'), may hold values from -0.5 to 0.5
- step: int32 [1], replicated, may hold values from 1 to 16
Outputs:
- merged: float32 [32, 512, 8192], P('replica', None, 'fsdp')
- momentum_next: float32 [512, 8192], P('replica', 'fsdp')
All inputs are finite; a program needn't handle non-finite values.
Results may differ from a plain program's by a relative error of at most 0.0003.
Values may be sent and summed in bfloat16 or wider, within the bound.
A program may use at most 64 MiB of HBM per device.

v0:
```python
import jax
import jax.numpy as jnp
from jax import lax
from jax.sharding import PartitionSpec as P

peak_rate = 0.25
warm_steps = 8.0
beta_one = 0.9
beta_two = 0.95
decay = 0.1
outer_rate = 0.7
outer_mu = 0.9
mix = 0.5


def per_device(
    features, cotangents, params, first_moment, second_moment, anchor, outer_momentum, step
):
    columns = lax.all_to_all(features, "fsdp", split_axis=1, concat_axis=0, tiled=True)
    grad = lax.dot_general(
        lax.all_gather(cotangents, "fsdp", axis=0, tiled=True),
        columns,
        (((0,), (0,)), ((), ())),
        preferred_element_type=jnp.float32,
    )
    t_value = step[0].astype(jnp.float32)
    rate = peak_rate * jnp.minimum(1.0, t_value / warm_steps)
    fix_one = 1.0 - jnp.power(jnp.float32(beta_one), t_value)
    fix_two = 1.0 - jnp.power(jnp.float32(beta_two), t_value)
    weight = params[0].astype(jnp.float32)
    moment_new = beta_one * first_moment[0].astype(jnp.float32) + (1.0 - beta_one) * grad
    second_new = beta_two * second_moment[0].astype(jnp.float32) + (1.0 - beta_two) * grad * grad
    update = moment_new / fix_one / (jnp.sqrt(second_new / fix_two) + 1e-08)
    local = weight - rate * (update + decay * weight)
    replicas = lax.axis_size("replica")
    total = lax.psum(local, "replica")
    anchor_whole, momentum_whole = (
        lax.all_gather(anchor, "replica", axis=0, tiled=True),
        lax.all_gather(outer_momentum, "replica", axis=0, tiled=True),
    )
    delta = anchor_whole - total / replicas
    momentum_full = outer_mu * momentum_whole + delta
    anchor_next = anchor_whole - outer_rate * (delta + outer_mu * momentum_full)
    share_rows = anchor.shape[0]
    momentum_next = lax.dynamic_slice_in_dim(
        momentum_full, lax.axis_index("replica") * share_rows, share_rows, 0
    )
    merged = mix * local + (1.0 - mix) * anchor_next
    return (merged[None], momentum_next)


def solution(mesh):
    in_specs = (
        P(("replica", "fsdp"), None),
        P(("replica", "fsdp"), None),
        P("replica", None, "fsdp"),
        P("replica", None, "fsdp"),
        P("replica", None, "fsdp"),
        P("replica", "fsdp"),
        P("replica", "fsdp"),
        P(),
    )
    out_specs = (P("replica", None, "fsdp"), P("replica", "fsdp"))
    return jax.shard_map(
        per_device, mesh=mesh, in_specs=in_specs, out_specs=out_specs, check_vma=False
    )
```

profile of v0, /device:TPU:1, one launch (start us, length us, event | category | flops | bytes accessed | tf_op | source)
XLA Modules:
  0.0 484.3 jit_solution(96954188703715856)
XLA Ops:
  7.2 0.0 all-gather.4.cloned.1.call-start
  7.2 0.7 all-gather.4.cloned.1.call-update
  7.9 4.1 copy.10
  12.0 10.2 %all-to-all-start = ((bf16[128,16,512]{0,2,1:T(8,128)(2,1)}), bf16[128,16,512]{0,2,1:T(8,128)(2,1)S(1)}, u32[]{:S(2)}, u32[]{:S(2)}) async-start(bf16[128,16,512]{0,2,1:T(8,128)(2,1)} %bitcast.24), calls=%async_computation | async-start | bytes 4194304 | tf_op jit(solution)/shard_map/all_to_all | solution.py:19
  22.2 0.0 all-gather.6.cloned.1.call-start
  22.2 0.7 all-gather.6.cloned.1.call-update
  22.9 0.0 all-gather.8.cloned.1.call-start
  23.0 0.7 all-gather.8.cloned.1.call-update
  23.7 0.0 all-reduce.2.cloned.1.call-start
  24.5 51.8 %all-to-all-done = bf16[128,16,512]{0,2,1:T(8,128)(2,1)S(1)} async-done(((bf16[128,16,512]{0,2,1:T(8,128)(2,1)}), bf16[128,16,512]{0,2,1:T(8,128)(2,1)S(1)}, u32[]{:S(2)}, u32[]{:S(2)}) %all-to-all-start) | async-done | bytes 2097184 | tf_op jit(solution)/shard_map/all_to_all | solution.py:19
  76.3 0.0 copy-start
  76.3 0.0 copy-start.1
  76.3 2.6 copy.11
  78.9 24.1 %all-gather.4.cloned.1.call-done = bf16[2048,512]{1,0:T(8,128)(2,1)} async-done(((bf16[128,512]{1,0:T(8,128)(2,1)}), bf16[2048,512]{1,0:T(8,128)(2,1)}) %all-gather.4.cloned.1.call-update) | async-done | bytes 2097168 | tf_op jit(solution)/shard_map/all_gather | solution.py:21
  103.0 0.0 copy-done
  103.0 0.0 copy-done.1
  103.0 5.3 %convert_subtract_fusion = f32[512,512]{1,0:T(8,128)} fusion(bf16[1,512,512]{2,1,0:T(8,128)(2,1)S(1)} %copy-done, bf16[1,512,512]{2,1,0:T(8,128)(2,1)S(1)} %copy-done.1, bf16[1,512,512]{2,1,0:T(8,128)(2,1)} %param.10, f32[]{:T(128)} %bitcast.8, f32[]{:T(128)} %bitcast.6, f32[]{:T(128)} %bitcast.1, bf16[2048,512]{1,0:T(8,128)(2,1)} %all-gather.4.cloned.1.call-done, ...), kind=kOutput, calls=%fused_computation.1 | convolution fusion | flops 1078460416 | bytes 6815756 | tf_op jit(solution)/shard_map/dot_general | solution.py:20
  108.3 0.0 all-reduce.2.cloned.1.call-update
  108.4 62.0 %all-gather.6.cloned.1.call-done = f32[512,512]{1,0:T(8,128)} async-done(((f32[16,512]{1,0:T(8,128)}), f32[512,512]{1,0:T(8,128)}) %all-gather.6.cloned.1.call-update) | async-done | bytes 1048592 | tf_op jit(solution)/shard_map/all_gather | solution.py:38
  170.3 68.3 %all-gather.8.cloned.1.call-done = f32[512,512]{1,0:T(8,128)} async-done(((f32[16,512]{1,0:T(8,128)}), f32[512,512]{1,0:T(8,128)}) %all-gather.8.cloned.1.call-update) | async-done | bytes 1048592 | tf_op jit(solution)/shard_map/all_gather | solution.py:39
  238.6 234.9 %all-reduce.2.cloned.1.call-done = f32[512,512]{1,0:T(8,128)} async-done(((f32[512,512]{1,0:T(8,128)}), f32[512,512]{1,0:T(8,128)}) %all-reduce.2.cloned.1.call-update) | async-done | bytes 1048592 | tf_op jit(solution)/shard_map/psum | solution.py:36
  473.5 3.7 multiply_add_fusion
  477.1 0.6 constant_dynamic-slice_fusion
Async XLA Ops:
  7.2 95.9 %all-gather.4.cloned.1.call-start = ((), (), s32[]{:S(2)}) async-start(), calls=%async_computation.1 | async-start | bytes 2228224 | tf_op jit(solution)/shard_map/all_gather | solution.py:21
  12.0 64.3 %all-to-all-start = ((bf16[128,16,512]{0,2,1:T(8,128)(2,1)}), bf16[128,16,512]{0,2,1:T(8,128)(2,1)S(1)}, u32[]{:S(2)}, u32[]{:S(2)}) async-start(bf16[128,16,512]{0,2,1:T(8,128)(2,1)} %bitcast.24), calls=%async_computation | async-start | bytes 4194304 | tf_op jit(solution)/shard_map/all_to_all | solution.py:19
  22.2 148.2 %all-gather.6.cloned.1.call-start = ((), (), s32[]{:S(2)}) async-start(), calls=%async_computation.2 | async-start | bytes 1081344 | tf_op jit(solution)/shard_map/all_gather | solution.py:38
  22.9 215.7 %all-gather.8.cloned.1.call-start = ((), (), s32[]{:S(2)}) async-start(), calls=%async_computation.4 | async-start | bytes 1081344 | tf_op jit(solution)/shard_map/all_gather | solution.py:39
  23.7 449.8 %all-reduce.2.cloned.1.call-start = ((), (), s32[]{:S(2)}) async-start(), calls=%async_computation.3 | async-start | bytes 2097152 | tf_op jit(solution)/shard_map/psum | solution.py:36
  76.3 26.8 %copy-start = (bf16[1,512,512]{2,1,0:T(8,128)(2,1)S(1)}, bf16[1,512,512]{2,1,0:T(8,128)(2,1)}, u32[]{:S(2)}) copy-start(bf16[1,512,512]{2,1,0:T(8,128)(2,1)} %param.12) | copy-start | bytes 1572868
  76.3 26.8 %copy-start.1 = (bf16[1,512,512]{2,1,0:T(8,128)(2,1)S(1)}, bf16[1,512,512]{2,1,0:T(8,128)(2,1)}, u32[]{:S(2)}) copy-start(bf16[1,512,512]{2,1,0:T(8,128)(2,1)} %param.11) | copy-start | bytes 1572868
Sparse Core Ops, SparseCore 0:
  11.0 91.9 all-gather.3
  105.2 65.1 all-gather.5
  172.5 66.0 all-gather.7
  242.0 231.4 all-reduce.1
where the time goes:
time: 485 us; the launch traced here: 484 us
  waiting for transfers between devices  443 us (91%)
  between operations  14.5 us (3%)
  starting transfers between devices  10.4 us (2%)
  local copies, waits for them, and re-layouts  7.29 us (2%)
  matrix products  5.29 us (1%)
    psum x1, waiting for transfers between devices, per_device(): total = lax.psum(local, 'replica')  235 us
    all_gather x1, waiting for transfers between devices, per_device(): lax.all_gather(outer_momentum, 'replica', axis=0, tiled=True)  68.3 us
    all_gather x1, waiting for transfers between devices, per_device(): lax.all_gather(anchor, 'replica', axis=0, tiled=True)  62 us
    all_to_all x1, waiting for transfers between devices, per_device(): lax.all_to_all(features, 'fsdp', split_axis=1, concat_axis=0, tiled=True)  51.8 us
    all_gather x1, waiting for transfers between devices, per_device(): lax.all_gather(cotangents, 'fsdp', axis=0, tiled=True)  24.1 us
    all_to_all x1, starting transfers between devices, per_device(): lax.all_to_all(features, 'fsdp', split_axis=1, concat_axis=0, tiled=True)  10.2 us
  transfers between devices with their start and end apart: 5, of which 5 were waited for; matrix products, arithmetic and copies ran while one was open for 2% of the time, Pallas kernels for 0%

commit v1 on v0

v1 whole, which is shorter than its diff:
```python
import functools
import math

import jax
import jax.numpy as jnp
from jax import lax
from jax.experimental import pallas as pl
from jax.experimental.pallas import tpu as pltpu
from jax.sharding import PartitionSpec as P

peak_rate = 0.25
warm_steps = 8.0
beta_one = 0.9
beta_two = 0.95
decay = 0.1
outer_rate = 0.7
outer_mu = 0.9
mix = 0.5

NX, NY, NZ = 4, 4, 8
CHUNKS = 4
F32, BF16 = jnp.float32, jnp.bfloat16


def kernel(
    nx, nz, nc,
    feats, cots, params, first, second, anchor, outer_momentum, step,
    merged_out, momentum_out,
    cot_own, cot_t, cot_all, fbuf, par, mom1, mom2, anc, outer,
    own, keep, s1, sd, se, r1, rd, r2,
    loc, rcore, ssum, rz, tot, ry, nxt, mout, momn,
    in_sem, feat_sem, cs, cr, xs, xr, ys, yr, ks, kr, zs, zr, ls, lr, os,
):
    ny = NY
    rows, width = par.shape
    cw = width // nc
    half = rows // 2
    tokens = feats.shape[0]
    slab = rows // nz
    rep = lax.axis_index("replica")
    fs = lax.axis_index("fsdp")
    core = lax.rem(rep, 2)
    yl = lax.rem(lax.div(rep, 2), 2)
    z = lax.div(rep, 4)
    x = lax.div(fs, ny)
    q = lax.rem(fs, ny)

    def at_fsdp(xx, qq):
        return {"fsdp": xx * ny + qq}

    def at_rep(zz, ll, cc):
        return {"replica": zz * 4 + ll * 2 + cc}

    x_peer = [at_fsdp(lax.rem(x + d, nx), q) for d in range(nx)]
    y_up = at_fsdp(x, lax.rem(q + 1, ny))
    y_down = at_fsdp(x, lax.rem(q + ny - 1, ny))
    z_of = [lax.rem(z + d, nz) for d in range(nz)]
    z_peer = [at_rep(zz, yl, core) for zz in z_of]
    core_peer = at_rep(z, yl, 1 - core)
    lo_peer = at_rep(z, 1 - yl, core)

    loads = []
    for k, (src, dst) in enumerate(
        [
            (cots, cot_own),
            (params.at[0], par),
            (first.at[0], mom1),
            (second.at[0], mom2),
            (anchor, anc),
            (outer_momentum, outer),
        ]
    ):
        loads.append(pltpu.make_async_copy(src, dst, in_sem.at[k]))
        loads[-1].start()

    barrier = pltpu.get_barrier_semaphore()
    peers = x_peer[1:] + [y_up, y_down] + z_peer[1:] + [core_peer, lo_peer]
    for peer in peers:
        pl.semaphore_signal(
            barrier, inc=1, device_id=peer, device_id_type=pl.DeviceIdType.MESH
        )

    def owner_cols(xx, o):
        return pl.multiple_of((xx * ny + lax.rem(q + o, ny)) * width, width)

    own_feats = []
    for o in range(ny):
        own_feats.append(
            pltpu.make_async_copy(
                feats.at[:, pl.ds(owner_cols(x, o), width)],
                fbuf.at[o, 0],
                feat_sem.at[o],
            )
        )
        own_feats[-1].start()

    sent = []

    def send(src, dst, ssem, rsem, peer):
        copy = pltpu.make_async_remote_copy(
            src_ref=src,
            dst_ref=dst,
            send_sem=ssem,
            recv_sem=rsem,
            device_id=peer,
            device_id_type=pl.DeviceIdType.MESH,
        )
        copy.start()
        sent.append(copy)
        return copy

    loads[0].wait()
    cot_t[...] = cot_own[...].T

    pl.semaphore_wait(barrier, len(peers))

    cot_copies = [
        send(
            cot_t,
            cot_all.at[:, d * tokens : (d + 1) * tokens],
            cs.at[d],
            cr.at[d],
            x_peer[d],
        )
        for d in range(1, nx)
    ]
    cot_all[:, 0:tokens] = cot_t[...]

    x_copies = {}

    def x_send(c, o):
        x_copies[c, o] = [
            send(
                feats.at[:, pl.ds(owner_cols(lax.rem(x + d, nx), o) + c * cw, cw)],
                fbuf.at[o, d, :, c * cw : (c + 1) * cw],
                xs.at[c, o, d],
                xr.at[c, o, d],
                x_peer[d],
            )
            for d in range(1, nx)
        ]

    def x_send_chunk(c):
        for o in (2, 1, 3, 0):
            x_send(c, o)

    def partial(c, o):
        if c == 0:
            own_feats[o].wait()
        for copy in x_copies[c, o]:
            copy.wait_recv()
        block = fbuf[o, :, :, c * cw : (c + 1) * cw].reshape(nx * tokens, cw)
        return jnp.dot(cot_all[...], block, preferred_element_type=F32)

    y_copies = {}

    def far(c):
        s1[c] = partial(c, 2).astype(BF16)
        y_copies[c, "1a"] = send(s1.at[c, :half], r1.at[c, :half], ys.at[c, 0], yr.at[c, 0], y_down)
        y_copies[c, "1b"] = send(s1.at[c, half:], r1.at[c, half:], ys.at[c, 1], yr.at[c, 1], y_up)

    def near(c):
        up = partial(c, 1)
        sd[c, :half] = up[:half].astype(BF16)
        y_copies[c, "da"] = send(sd.at[c, :half], rd.at[c, :half], ys.at[c, 2], yr.at[c, 2], y_up)
        keep[c, half:] = up[half:]
        down = partial(c, 3)
        sd[c, half:] = down[half:].astype(BF16)
        y_copies[c, "db"] = send(sd.at[c, half:], rd.at[c, half:], ys.at[c, 3], yr.at[c, 3], y_down)
        keep[c, :half] = down[:half]

    def mine(c):
        own[c] = partial(c, 0)

    def relay(c):
        y_copies[c, "1a"].wait_recv()
        se[c, :half] = (keep[c, :half] + r1[c, :half].astype(F32)).astype(BF16)
        y_copies[c, "2a"] = send(se.at[c, :half], r2.at[c, :half], ys.at[c, 4], yr.at[c, 4], y_down)
        y_copies[c, "1b"].wait_recv()
        se[c, half:] = (keep[c, half:] + r1[c, half:].astype(F32)).astype(BF16)
        y_copies[c, "2b"] = send(se.at[c, half:], r2.at[c, half:], ys.at[c, 5], yr.at[c, 5], y_up)

    rep_copies = {}

    def adam(c):
        if c == 0:
            for k in (1, 2, 3):
                loads[k].wait()
        for name in ("da", "db", "2a", "2b"):
            y_copies[c, name].wait_recv()
        t_value = jnp.full((1, cw), step[0].astype(F32), F32)
        rate = peak_rate * jnp.minimum(1.0, t_value / warm_steps)
        inv_one = 1.0 / (1.0 - jnp.exp(t_value * math.log(beta_one)))
        inv_two = 1.0 / (1.0 - jnp.exp(t_value * math.log(beta_two)))
        cols = slice(c * cw, (c + 1) * cw)

        def body(k, carry):
            here = pl.ds(pl.multiple_of(k * slab, slab), slab)
            grad = own[c, here] + rd[c, here].astype(F32) + r2[c, here].astype(F32)
            weight = par[here, cols].astype(F32)
            m = beta_one * mom1[here, cols].astype(F32) + (1.0 - beta_one) * grad
            v = beta_two * mom2[here, cols].astype(F32) + (1.0 - beta_two) * grad * grad
            update = (m * inv_one) / (jnp.sqrt(v * inv_two) + 1e-08)
            new = weight - rate * (update + decay * weight)
            new = new.reshape(2, 2, slab // 4, cw)
            loc[c, 0, k] = new[:, 0]
            loc[c, 1, k] = new[:, 1]
            return carry

        lax.fori_loop(0, nz, body, 0)
        rep_copies[c, "core"] = send(
            loc.at[c, 1 - core], rcore.at[c], ks.at[c, 0], kr.at[c, 0], core_peer
        )

    def z_reduce(c):
        rep_copies[c, "core"].wait_recv()
        copies = []
        for d in list(range(1, nz)) + [0]:
            zz = z_of[d]
            ssum[c, zz] = loc[c, core, zz] + rcore[c, zz]
            if d:
                copies.append(
                    send(ssum.at[c, zz], rz.at[c, d], zs.at[c, 0, d], zr.at[c, 0, d], z_peer[d])
                )
        rep_copies[c, "z"] = copies

    def lo_reduce(c):
        total = ssum[c, z]
        for d, copy in enumerate(rep_copies[c, "z"], 1):
            copy.wait_recv()
            total = total + rz[c, d]
        tot[c] = total
        rep_copies[c, "lo"] = send(
            tot.at[c, 1 - yl], ry.at[c], ls.at[c, 0], lr.at[c, 0], lo_peer
        )

    def outer_step(c):
        if c == 0:
            loads[4].wait()
            loads[5].wait()
        cols = slice(c * cw, (c + 1) * cw)
        rep_copies[c, "lo"].wait_recv()
        old = anc[:, cols]
        delta = old - (tot[c, yl] + ry[c]) * (1.0 / (4 * nz))
        momentum = outer_mu * outer[:, cols] + delta
        momn[:, cols] = momentum
        nxt[c, core, z, yl] = old - outer_rate * (delta + outer_mu * momentum)
        piece = nxt.at[c, core, z, yl]
        rep_copies[c, "lo2"] = send(piece, piece, ls.at[c, 1], lr.at[c, 1], lo_peer)

    def z_gather(c):
        rep_copies[c, "lo2"].wait_recv()
        piece = nxt.at[c, core, z]
        rep_copies[c, "z2"] = [
            send(piece, piece, zs.at[c, 1, d], zr.at[c, 1, d], z_peer[d])
            for d in range(1, nz)
        ]

    def core_gather(c):
        for copy in rep_copies[c, "z2"]:
            copy.wait_recv()
        piece = nxt.at[c, core]
        rep_copies[c, "core2"] = send(piece, piece, ks.at[c, 1], kr.at[c, 1], core_peer)

    out_copies = []

    def merge(c):
        rep_copies[c, "core2"].wait_recv()

        def body(k, carry):
            here = pl.ds(pl.multiple_of(k * slab, slab), slab)
            both = [mix * loc[c, j, k] + (1.0 - mix) * nxt[c, j, k] for j in (0, 1)]
            mout[c, here] = jnp.stack(both, axis=1).reshape(slab, cw)
            return carry

        lax.fori_loop(0, nz, body, 0)
        copy = pltpu.make_async_copy(
            mout.at[c], merged_out.at[0, :, c * cw : (c + 1) * cw], os.at[c]
        )
        copy.start()
        out_copies.append(copy)

    x_send_chunk(0)
    if nc > 1:
        x_send_chunk(1)
    for copy in cot_copies:
        copy.wait_recv()
    stages = [
        ("far", 0, far), ("x", 0, None), ("near", 0, near), ("mine", 0, mine),
        ("lo_reduce", 2, lo_reduce), ("core_gather", 3, core_gather),
        ("adam", 1, adam), ("outer", 2, outer_step), ("relay", 0, relay),
        ("z_reduce", 1, z_reduce), ("z_gather", 2, z_gather), ("merge", 3, merge),
    ]
    for k in range(nc + 3):
        for name, lag, stage in stages:
            c = k - lag
            if not 0 <= c < nc:
                continue
            if name == "x":
                if c + 2 < nc:
                    x_send_chunk(c + 2)
            else:
                stage(c)

    momentum_copy = pltpu.make_async_copy(momn, momentum_out, os.at[nc])
    momentum_copy.start()
    for copy in sent:
        copy.wait_send()
    for copy in out_copies:
        copy.wait()
    momentum_copy.wait()


def per_device(features, cotangents, params, first, second, anchor, outer_momentum, step, *, nx, nz, nc):
    tokens = features.shape[0]
    rows, width = params.shape[1:]
    cw = width // nc
    piece = anchor.shape[0]
    hbm = pl.BlockSpec(memory_space=pl.ANY)
    dma = pltpu.SemaphoreType.DMA
    return pl.pallas_call(
        functools.partial(kernel, nx, nz, nc),
        out_shape=(
            jax.ShapeDtypeStruct((1, rows, width), F32),
            jax.ShapeDtypeStruct((piece, width), F32),
        ),
        in_specs=[hbm] * 7 + [pl.BlockSpec(memory_space=pltpu.SMEM)],
        out_specs=(hbm, hbm),
        scratch_shapes=[
            pltpu.VMEM((tokens, rows), BF16),
            pltpu.VMEM((rows, tokens), BF16),
            pltpu.VMEM((rows, nx * tokens), BF16),
            pltpu.VMEM((NY, nx, tokens, width), BF16),
            pltpu.VMEM((rows, width), BF16),
            pltpu.VMEM((rows, width), BF16),
            pltpu.VMEM((rows, width), BF16),
            pltpu.VMEM((piece, width), F32),
            pltpu.VMEM((piece, width), F32),
            pltpu.VMEM((nc, rows, cw), F32),
            pltpu.VMEM((nc, rows, cw), F32),
            pltpu.VMEM((nc, rows, cw), BF16),
            pltpu.VMEM((nc, rows, cw), BF16),
            pltpu.VMEM((nc, rows, cw), BF16),
            pltpu.VMEM((nc, rows, cw), BF16),
            pltpu.VMEM((nc, rows, cw), BF16),
            pltpu.VMEM((nc, rows, cw), BF16),
            pltpu.VMEM((nc, 2, nz, 2, piece, cw), F32),
            pltpu.VMEM((nc, nz, 2, piece, cw), F32),
            pltpu.VMEM((nc, nz, 2, piece, cw), F32),
            pltpu.VMEM((nc, nz, 2, piece, cw), F32),
            pltpu.VMEM((nc, 2, piece, cw), F32),
            pltpu.VMEM((nc, piece, cw), F32),
            pltpu.VMEM((nc, 2, nz, 2, piece, cw), F32),
            pltpu.VMEM((nc, rows, cw), F32),
            pltpu.VMEM((piece, width), F32),
            dma((6,)), dma((NY,)),
            dma((nx,)), dma((nx,)),
            dma((nc, NY, nx)), dma((nc, NY, nx)),
            dma((nc, 6)), dma((nc, 6)),
            dma((nc, 2)), dma((nc, 2)),
            dma((nc, 2, nz)), dma((nc, 2, nz)),
            dma((nc, 2)), dma((nc, 2)),
            dma((nc + 1,)),
        ],
        compiler_params=pltpu.CompilerParams(
            collective_id=0, has_side_effects=True, vmem_limit_bytes=48 * 1024 * 1024
        ),
    )(features, cotangents, params, first, second, anchor, outer_momentum, step)


def build(mesh, nx, nz, nc):
    in_specs = (
        P(("replica", "fsdp"), None),
        P(("replica", "fsdp"), None),
        P("replica", None, "fsdp"),
        P("replica", None, "fsdp"),
        P("replica", None, "fsdp"),
        P("replica", "fsdp"),
        P("replica", "fsdp"),
        P(),
    )
    out_specs = (P("replica", None, "fsdp"), P("replica", "fsdp"))
    return jax.shard_map(
        functools.partial(per_device, nx=nx, nz=nz, nc=nc),
        mesh=mesh, in_specs=in_specs, out_specs=out_specs, check_vma=False,
    )


def solution(mesh):
    return build(mesh, NX, NZ, CHUNKS)
```

time: 485 us -> 107 us (0.22)
  waiting for transfers between devices: 443 us -> 0 us
  Pallas kernels: 0 us -> 95.5 us
  between operations: 14.5 us -> 1.3 us
  starting transfers between devices: 10.4 us -> 0 us
  matrix products: 5.29 us -> 0 us
    psum x1 -> x0, waiting for transfers between devices: 235 us -> none  [per_device(): total = lax.psum(local, 'replica')]
    all_gather x3 -> x0, waiting for transfers between devices: 154 us -> none  [the longest x1 68.3 us: per_device(): lax.all_gather(outer_momentum, 'replica', axis=0, tiled=True)]
    pallas_call x0 -> x1, Pallas kernels: none -> 95.5 us  [per_device(): pl.pallas_call(functools.partial(kernel, nx, nz, nc), out_shape=(jax.Shap...]
    all_to_all x1 -> x0, waiting for transfers between devices: 51.8 us -> none  [per_device(): lax.all_to_all(features, 'fsdp', split_axis=1, concat_axis=0, tiled=True)]
    all_to_all x1 -> x0, starting transfers between devices: 10.2 us -> none  [per_device(): lax.all_to_all(features, 'fsdp', split_axis=1, concat_axis=0, tiled=True)]
    dot_general x1 -> x0, matrix products: 5.29 us -> none  [per_device(): lax.dot_general(lax.all_gather(cotangents, 'fsdp', axis=0, tiled=True), c...]
  transfers between devices with their start and end apart: 5 -> 0, of which waited for: 5 -> 0; matrix products, arithmetic and copies ran while one was open for 2% -> 0% of each run, Pallas kernels for 0% -> 0%
where the time goes in v1:
time: 107 us; the launch traced here: 105 us
  Pallas kernels  95.5 us (89%)
  local copies, waits for them, and re-layouts  8.71 us (8%)
  between operations  1.3 us (1%)
    pallas_call x1, Pallas kernels, per_device(): pl.pallas_call(functools.partial(kernel, nx, nz, nc), out_shape=(jax.Shap...  95.5 us
    unnamed x16, local copies, waits for them, and re-layouts  8.71 us

profile of v1, /device:TPU:1, one launch (start us, length us, event | category | flops | bytes accessed | tf_op | source)
XLA Modules:
  0.0 105.5 jit_solution(1971691158679396191)
XLA Ops:
  1.3 0.0 copy-start
  1.3 1.6 %copy-done = bf16[128,8192]{1,0:T(8,128)(2,1)S(1)} copy-done((bf16[128,8192]{1,0:T(8,128)(2,1)S(1)}, bf16[128,8192]{1,0:T(8,128)(2,1)}, u32[]{:S(2)}) %copy-start) | copy-done | bytes 2097176
  2.9 0.0 copy-start.1
  2.9 1.0 copy-done.1
  3.9 0.0 copy-start.2
  3.9 1.0 copy-done.2
  5.0 0.0 copy-start.3
  5.0 1.0 copy-done.3
  6.0 0.0 copy-start.4
  6.0 0.9 copy-done.4
  6.9 0.0 copy-start.5
  6.9 0.8 copy-done.5
  7.7 0.0 copy-start.6
  7.7 0.8 copy-done.6
  8.4 95.5 %shard_map.95 = (f32[1,512,512]{2,1,0:T(8,128)S(1)}, f32[16,512]{1,0:T(8,128)S(1)}) custom-call(bf16[128,8192]{1,0:T(8,128)(2,1)S(1)} %copy-done, bf16[128,512]{1,0:T(8,128)(2,1)S(1)} %copy-done.4, bf16[1,512,512]{2,1,0:T(8,128)(2,1)S(1)} %copy-done.1, bf16[1,512,512]{2,1,0:T(8,128)(2,1)S(1)} %copy-done.2, bf16[1,512,512]{2,1,0:T(8,128)(2,1)S(1)} %copy-done.3, ...), custom_call_target="tpu_custom_call" | custom-call | tf_op jit(solution)/shard_map/pallas_call | solution.py:321
  103.9 1.0 copy.13
  104.9 0.6 copy.14
Async XLA Ops:
  1.3 1.6 %copy-start = (bf16[128,8192]{1,0:T(8,128)(2,1)S(1)}, bf16[128,8192]{1,0:T(8,128)(2,1)}, u32[]{:S(2)}) copy-start(bf16[128,8192]{1,0:T(8,128)(2,1)} %feats.1) | copy-start | bytes 6291460
  2.9 1.0 copy-start.1
  3.9 1.0 copy-start.2
  5.0 1.0 copy-start.3
  6.0 0.9 copy-start.4
  6.9 0.8 copy-start.5
  7.7 0.8 copy-start.6

commit v2 on v1

v2 whole, which is shorter than its diff:
```python
import functools
import math

import jax
import jax.numpy as jnp
from jax import lax
from jax.experimental import pallas as pl
from jax.experimental.pallas import tpu as pltpu
from jax.sharding import PartitionSpec as P

peak_rate = 0.25
warm_steps = 8.0
beta_one = 0.9
beta_two = 0.95
decay = 0.1
outer_rate = 0.7
outer_mu = 0.9
mix = 0.5

NX, NY, NZ = 4, 4, 8
CHUNKS = 4
AHEAD = 2
F32, BF16 = jnp.float32, jnp.bfloat16


def kernel(
    nx, nz, nc,
    feats, cots, params, first, second, anchor, outer_momentum, step,
    merged_out, momentum_out,
    cot_own, cot_t, cot_all, fbuf, par, mom1, mom2, anc, outer,
    own, keep, s1, sd, se, r1, rd, r2,
    loc, rcore, ssum, rz, tot, ry, nxt, mout, momn,
    step_v, in_sem, feat_sem, cs, cr, xs, xr, ys, yr, ks, kr, os_, zs, zr, ls, lr, os,
):
    ny = NY
    rows, width = par.shape
    cw = width // nc
    half = rows // 2
    tokens = feats.shape[0]
    slab = rows // nz
    rep = lax.axis_index("replica")
    fs = lax.axis_index("fsdp")
    core = lax.rem(rep, 2)
    yl = lax.rem(lax.div(rep, 2), 2)
    z = lax.div(rep, 4)
    x = lax.div(fs, ny)
    q = lax.rem(fs, ny)

    def at_fsdp(xx, qq):
        return {"fsdp": xx * ny + qq}

    def at_rep(zz, ll, cc):
        return {"replica": zz * 4 + ll * 2 + cc}

    x_peer = [at_fsdp(lax.rem(x + d, nx), q) for d in range(nx)]
    y_up = at_fsdp(x, lax.rem(q + 1, ny))
    y_down = at_fsdp(x, lax.rem(q + ny - 1, ny))
    z_of = [lax.rem(z + d, nz) for d in range(nz)]
    z_peer = [[at_rep(zz, yl, core), at_rep(zz, 1 - yl, core)] for zz in z_of]
    core_peer = at_rep(z, yl, 1 - core)
    lo_peer = z_peer[0][1]

    loads = []
    for k, (src, dst) in enumerate(
        [
            (cots, cot_own),
            (params.at[0], par),
            (first.at[0], mom1),
            (second.at[0], mom2),
            (anchor, anc.at[yl]),
            (outer_momentum, outer.at[yl]),
            (step, step_v),
        ]
    ):
        loads.append(pltpu.make_async_copy(src, dst, in_sem.at[k]))
        loads[-1].start()

    barrier = pltpu.get_barrier_semaphore()
    peers = x_peer[1:] + [y_up, y_down, core_peer] + [p for d in range(nz) for p in z_peer[d]][1:]
    for peer in peers:
        pl.semaphore_signal(
            barrier, inc=1, device_id=peer, device_id_type=pl.DeviceIdType.MESH
        )

    def owner_cols(xx, o):
        return pl.multiple_of((xx * ny + lax.rem(q + o, ny)) * width, width)

    own_feats = []
    for o in range(ny):
        own_feats.append(
            pltpu.make_async_copy(
                feats.at[:, pl.ds(owner_cols(x, o), width)],
                fbuf.at[o, 0],
                feat_sem.at[o],
            )
        )
        own_feats[-1].start()

    sent = []

    def send(src, dst, ssem, rsem, peer):
        copy = pltpu.make_async_remote_copy(
            src_ref=src,
            dst_ref=dst,
            send_sem=ssem,
            recv_sem=rsem,
            device_id=peer,
            device_id_type=pl.DeviceIdType.MESH,
        )
        copy.start()
        sent.append(copy)
        return copy

    loads[0].wait()
    cot_t[...] = cot_own[...].T

    pl.semaphore_wait(barrier, len(peers))

    cot_copies = {}

    def cot_send(h):
        some = slice(h * half, (h + 1) * half)
        cot_copies[h] = [
            send(
                cot_t.at[some],
                cot_all.at[some, d * tokens : (d + 1) * tokens],
                cs.at[h, d],
                cr.at[h, d],
                x_peer[d],
            )
            for d in range(1, nx)
        ]

    cot_all[:, 0:tokens] = cot_t[...]
    outer_copies = [
        send(src, dst.at[yl], os_.at[0, k], os_.at[1, k], lo_peer)
        for k, (src, dst) in enumerate([(anchor, anc), (outer_momentum, outer)])
    ]

    x_copies = {}

    def x_send(c, o):
        x_copies[c, o] = [
            send(
                feats.at[:, pl.ds(owner_cols(lax.rem(x + d, nx), o) + c * cw, cw)],
                fbuf.at[o, d, :, c * cw : (c + 1) * cw],
                xs.at[c, o, d],
                xr.at[c, o, d],
                x_peer[d],
            )
            for d in range(1, nx)
        ]

    x_order = [(c + 1 if o == 2 else c, o) for c in range(-1, nc) for o in (2, 1, 3, 0)]
    x_order = [(c, o) for c, o in x_order if 0 <= c < nc]
    x_done = [0]

    def x_ahead(c, o, more=AHEAD):
        upto = min(x_order.index((c, o)) + 1 + more, len(x_order))
        for at in range(x_done[0], upto):
            x_send(*x_order[at])
        x_done[0] = max(x_done[0], upto)

    def block(c, o):
        x_ahead(c, o)
        if c == 0:
            own_feats[o].wait()
        for copy in x_copies[c, o]:
            copy.wait_recv()
        return fbuf[o, :, :, c * cw : (c + 1) * cw].reshape(nx * tokens, cw)

    halves = (slice(0, half), slice(half, rows))

    def dot(h, cols):
        for copy in cot_copies.pop(h, []):
            copy.wait_recv()
        return jnp.dot(cot_all[halves[h]], cols, preferred_element_type=F32)

    y_copies = {}

    def y_send(c, k, h, src, dst, peer):
        y_copies[c, k] = send(
            src.at[c, halves[h]], dst.at[c, halves[h]], ys.at[c, k], yr.at[c, k], peer
        )

    def far(c):
        cols = block(c, 2)
        for h, peer in ((0, y_down), (1, y_up)):
            s1[c, halves[h]] = dot(h, cols).astype(BF16)
            y_send(c, h, h, s1, r1, peer)

    def near(c):
        cols = block(c, 1)
        sd[c, :half] = dot(0, cols).astype(BF16)
        y_send(c, 2, 0, sd, rd, y_up)
        keep[c, half:] = dot(1, cols)
        cols = block(c, 3)
        sd[c, half:] = dot(1, cols).astype(BF16)
        y_send(c, 3, 1, sd, rd, y_down)
        keep[c, :half] = dot(0, cols)

    def relay(c):
        for h, peer in ((0, y_down), (1, y_up)):
            y_copies[c, h].wait_recv()
            se[c, halves[h]] = (keep[c, halves[h]] + r1[c, halves[h]].astype(F32)).astype(BF16)
            y_send(c, 4 + h, h, se, r2, peer)

    def mine(c):
        cols = block(c, 0)
        for h in (0, 1):
            own[c, halves[h]] = dot(h, cols)

    rep_copies = {}

    def adam(c):
        if c == 0:
            for k in (1, 2, 3, 6):
                loads[k].wait()
        for k in (2, 3, 4, 5):
            y_copies[c, k].wait_recv()
        t_value = jnp.full((1, cw), step_v[0].astype(F32), F32)
        rate = peak_rate * jnp.minimum(1.0, t_value / warm_steps)
        inv_one = 1.0 / (1.0 - jnp.exp(t_value * math.log(beta_one)))
        inv_two = 1.0 / (1.0 - jnp.exp(t_value * math.log(beta_two)))
        cols = slice(c * cw, (c + 1) * cw)

        def body(k, carry):
            here = pl.ds(pl.multiple_of(k * slab, slab), slab)
            grad = own[c, here] + rd[c, here].astype(F32) + r2[c, here].astype(F32)
            weight = par[here, cols].astype(F32)
            m = beta_one * mom1[here, cols].astype(F32) + (1.0 - beta_one) * grad
            v = beta_two * mom2[here, cols].astype(F32) + (1.0 - beta_two) * grad * grad
            update = (m * inv_one) / (jnp.sqrt(v * inv_two) + 1e-08)
            new = weight - rate * (update + decay * weight)
            new = new.reshape(2, 2, slab // 4, cw)
            loc[c, 0, k] = new[:, 0]
            loc[c, 1, k] = new[:, 1]
            return carry

        lax.fori_loop(0, nz, body, 0)
        rep_copies[c, "core"] = send(
            loc.at[c, 1 - core], rcore.at[c], ks.at[c, 0], kr.at[c, 0], core_peer
        )

    straight = [c == nc - 1 for c in range(nc)]

    def z_reduce(c):
        rep_copies[c, "core"].wait_recv()
        copies = []
        for d in list(range(1, nz)) + [0]:
            zz = z_of[d]
            ssum[c, zz] = loc[c, core, zz] + rcore[c, zz]
            if straight[c]:
                for e in (0, 1):
                    if d or e:
                        lo = 1 - yl if e else yl
                        copies.append(
                            send(ssum.at[c, zz, lo], rz.at[c, d, e], zs.at[c, 0, d, e], zr.at[c, 0, d, e], z_peer[d][e])
                        )
            elif d:
                copies.append(
                    send(ssum.at[c, zz], rz.at[c, d], zs.at[c, 0, d, 0], zr.at[c, 0, d, 0], z_peer[d][0])
                )
        rep_copies[c, "z"] = copies

    def lo_reduce(c):
        for copy in rep_copies[c, "z"]:
            copy.wait_recv()
        if straight[c]:
            total = ssum[c, z, yl] + rz[c, 0, 1]
            for d in range(1, nz):
                total = total + (rz[c, d, 0] + rz[c, d, 1])
            tot[c, 0] = total
        else:
            total = ssum[c, z]
            for d in range(1, nz):
                total = total + rz[c, d]
            tot[c] = total
            rep_copies[c, "lo"] = send(tot.at[c], ry.at[c], ls.at[c], lr.at[c], lo_peer)

    def outer_step(c):
        cols = slice(c * cw, (c + 1) * cw)
        if straight[c]:
            total, rows_of = tot[c, 0], yl
        else:
            rep_copies[c, "lo"].wait_recv()
            total, rows_of = tot[c] + ry[c], slice(None)
        old = anc[rows_of, :, cols]
        delta = old - total * (1.0 / (4 * nz))
        momentum = outer_mu * outer[rows_of, :, cols] + delta
        nxt[c, core, z, rows_of] = old - outer_rate * (delta + outer_mu * momentum)
        piece = nxt.at[c, core, z, yl] if straight[c] else nxt.at[c, core, z]
        rep_copies[c, "z2"] = [
            send(piece, piece, zs.at[c, 1, d, e], zr.at[c, 1, d, e], z_peer[d][e])
            for d in range(nz)
            for e in ((0, 1) if straight[c] else (0,))
            if d or e
        ]
        momn[rows_of, :, cols] = momentum

    def core_gather(c):
        for copy in rep_copies[c, "z2"]:
            copy.wait_recv()
        piece = nxt.at[c, core]
        rep_copies[c, "core2"] = send(piece, piece, ks.at[c, 1], kr.at[c, 1], core_peer)

    out_copies = []

    def merge(c):
        rep_copies[c, "core2"].wait_recv()

        def body(k, carry):
            here = pl.ds(pl.multiple_of(k * slab, slab), slab)
            both = [mix * loc[c, j, k] + (1.0 - mix) * nxt[c, j, k] for j in (0, 1)]
            mout[c, here] = jnp.stack(both, axis=1).reshape(slab, cw)
            return carry

        lax.fori_loop(0, nz, body, 0)
        copy = pltpu.make_async_copy(
            mout.at[c], merged_out.at[0, :, c * cw : (c + 1) * cw], os.at[c]
        )
        copy.start()
        out_copies.append(copy)

    cot_send(0)
    x_ahead(*x_order[0])
    cot_send(1)
    far(0)
    for k in range(nc + 1):
        if k + 1 < nc:
            far(k + 1)
        if k < nc:
            near(k)
            relay(k)
            mine(k)
        if k + 1 < nc:
            x_ahead(k + 1, 0, 0)
        if k == 2:
            for copy in loads[4:6]:
                copy.wait()
            for copy in outer_copies:
                copy.wait_recv()
        stages = [(outer_step, 3), (core_gather, 4), (lo_reduce, 2), (merge, 4), (adam, 1), (z_reduce, 1)]
        for stage, lag in stages:
            if 0 <= k - lag < nc:
                stage(k - lag)
    c = nc - 1
    for stage, lag in [
        (outer_step, 1), (core_gather, 2), (merge, 2), (lo_reduce, 0), (outer_step, 0),
        (core_gather, 1), (merge, 1), (core_gather, 0), (merge, 0),
    ]:
        stage(c - lag)

    momentum_copy = pltpu.make_async_copy(momn.at[yl], momentum_out, os.at[nc])
    momentum_copy.start()
    for copy in sent:
        copy.wait_send()
    for copy in out_copies:
        copy.wait()
    momentum_copy.wait()


def per_device(features, cotangents, params, first, second, anchor, outer_momentum, step, *, nx, nz, nc):
    tokens = features.shape[0]
    rows, width = params.shape[1:]
    cw = width // nc
    piece = anchor.shape[0]
    hbm = pl.BlockSpec(memory_space=pl.ANY)
    dma = pltpu.SemaphoreType.DMA
    operands = [
        pltpu.with_memory_space_constraint(a, pltpu.HBM)
        for a in (features, cotangents, params, first, second, anchor, outer_momentum)
    ]
    return pl.pallas_call(
        functools.partial(kernel, nx, nz, nc),
        out_shape=(
            jax.ShapeDtypeStruct((1, rows, width), F32),
            jax.ShapeDtypeStruct((piece, width), F32),
        ),
        in_specs=[hbm] * 8,
        out_specs=(hbm, hbm),
        scratch_shapes=[
            pltpu.VMEM((tokens, rows), BF16),
            pltpu.VMEM((rows, tokens), BF16),
            pltpu.VMEM((rows, nx * tokens), BF16),
            pltpu.VMEM((NY, nx, tokens, width), BF16),
            pltpu.VMEM((rows, width), BF16),
            pltpu.VMEM((rows, width), BF16),
            pltpu.VMEM((rows, width), BF16),
            pltpu.VMEM((2, piece, width), F32),
            pltpu.VMEM((2, piece, width), F32),
            pltpu.VMEM((nc, rows, cw), F32),
            pltpu.VMEM((nc, rows, cw), F32),
            pltpu.VMEM((nc, rows, cw), BF16),
            pltpu.VMEM((nc, rows, cw), BF16),
            pltpu.VMEM((nc, rows, cw), BF16),
            pltpu.VMEM((nc, rows, cw), BF16),
            pltpu.VMEM((nc, rows, cw), BF16),
            pltpu.VMEM((nc, rows, cw), BF16),
            pltpu.VMEM((nc, 2, nz, 2, piece, cw), F32),
            pltpu.VMEM((nc, nz, 2, piece, cw), F32),
            pltpu.VMEM((nc, nz, 2, piece, cw), F32),
            pltpu.VMEM((nc, nz, 2, piece, cw), F32),
            pltpu.VMEM((nc, 2, piece, cw), F32),
            pltpu.VMEM((nc, 2, piece, cw), F32),
            pltpu.VMEM((nc, 2, nz, 2, piece, cw), F32),
            pltpu.VMEM((nc, rows, cw), F32),
            pltpu.VMEM((2, piece, width), F32),
            pltpu.SMEM((1,), jnp.int32),
            dma((7,)), dma((NY,)),
            dma((2, nx)), dma((2, nx)),
            dma((nc, NY, nx)), dma((nc, NY, nx)),
            dma((nc, 6)), dma((nc, 6)),
            dma((nc, 2)), dma((nc, 2)),
            dma((2, 2)),
            dma((nc, 2, nz, 2)), dma((nc, 2, nz, 2)),
            dma((nc,)), dma((nc,)),
            dma((nc + 1,)),
        ],
        compiler_params=pltpu.CompilerParams(
            collective_id=0, has_side_effects=True, vmem_limit_bytes=48 * 1024 * 1024
        ),
    )(*operands, step)


def build(mesh, nx, nz, nc):
    in_specs = (
        P(("replica", "fsdp"), None),
        P(("replica", "fsdp"), None),
        P("replica", None, "fsdp"),
        P("replica", None, "fsdp"),
        P("replica", None, "fsdp"),
        P("replica", "fsdp"),
        P("replica", "fsdp"),
        P(),
    )
    out_specs = (P("replica", None, "fsdp"), P("replica", "fsdp"))
    return jax.shard_map(
        functools.partial(per_device, nx=nx, nz=nz, nc=nc),
        mesh=mesh, in_specs=in_specs, out_specs=out_specs, check_vma=False,
    )


def solution(mesh):
    return build(mesh, NX, NZ, CHUNKS)
```

time: 107 us -> 90.9 us (0.85); the launches traced: 105 us -> 90.7 us
  Pallas kernels: 95.5 us -> 87.8 us
  local copies, waits for them, and re-layouts: 8.71 us -> 1.59 us
    pallas_call x1, Pallas kernels: 95.5 us -> 87.8 us  [per_device(): pl.pallas_call(functools.partial(kernel, nx, nz, nc), out_shape=(jax.Shap...]
    unnamed x16 -> x2, local copies, waits for them, and re-layouts: 8.71 us -> 1.59 us
where the time goes in v2:
time: 90.9 us; the launch traced here: 90.7 us
  Pallas kernels  87.8 us (97%)
  local copies, waits for them, and re-layouts  1.59 us (2%)
  between operations  1.29 us (1%)
    pallas_call x1, Pallas kernels, per_device(): pl.pallas_call(functools.partial(kernel, nx, nz, nc), out_shape=(jax.Shap...  87.8 us

profile of v2, /device:TPU:1, one launch (start us, length us, event | category | flops | bytes accessed | tf_op | source)
XLA Modules:
  0.0 90.7 jit_solution(10471594128705504513)
XLA Ops:
  1.3 87.8 %shard_map.95 = (f32[1,512,512]{2,1,0:T(8,128)S(1)}, f32[16,512]{1,0:T(8,128)S(1)}) custom-call(bf16[128,8192]{1,0:T(8,128)(2,1)} %feats.1, bf16[128,512]{1,0:T(8,128)(2,1)} %cots.1, bf16[1,512,512]{2,1,0:T(8,128)(2,1)} %params.1, bf16[1,512,512]{2,1,0:T(8,128)(2,1)} %first.1, bf16[1,512,512]{2,1,0:T(8,128)(2,1)} %second.1, f32[16,512]{1,0:T(8,128)} %anchor.1, ...), custom_call_target="tpu_custom_call" | custom-call | tf_op jit(solution)/shard_map/pallas_call | solution.py:374
  89.1 1.0 %copy.13 = f32[1,512,512]{2,1,0:T(8,128)} copy(f32[1,512,512]{2,1,0:T(8,128)S(1)} %get-tuple-element.4) | data formatting | bytes 2097152
  90.1 0.6 copy.14

commit v3 on v2

v3 whole, which is shorter than its diff:
```python
import functools
import math

import jax
import jax.numpy as jnp
from jax import lax
from jax.experimental import pallas as pl
from jax.experimental.pallas import tpu as pltpu
from jax.sharding import PartitionSpec as P

peak_rate = 0.25
warm_steps = 8.0
beta_one = 0.9
beta_two = 0.95
decay = 0.1
outer_rate = 0.7
outer_mu = 0.9
mix = 0.5

NX, NY, NZ = 4, 4, 8
CHUNKS = 4
SUB = 8
F32, BF16 = jnp.float32, jnp.bfloat16


def kernel(
    nx, nz, nc, y_units, r_units, straight,
    feats, cots, params, first, second, anchor, outer_momentum, step,
    merged_out, momentum_out,
    cot_own, cot_t, cot_all, fbuf, par, mom1, mom2, anc, outer,
    own, keep, s1, sd, se, r1, rd, r2,
    loc, rcore, ssum, rz, tot, ry, nxt, mout, momn,
    step_v, in_sem, feat_sem, cs, cr, xs, xr, ys, yr, ks, kr, os_, zs, zr, ls, lr, os,
):
    ny = NY
    rows, width = par.shape
    cw = width // nc
    tokens = feats.shape[0]
    slab = rows // nz
    part = rows // 2
    quarter = rows // 4
    rep = lax.axis_index("replica")
    fs = lax.axis_index("fsdp")
    core = lax.rem(rep, 2)
    yl = lax.rem(lax.div(rep, 2), 2)
    z = lax.div(rep, 4)
    x = lax.div(fs, ny)
    q = lax.rem(fs, ny)

    def at_fsdp(xx, qq):
        return {"fsdp": xx * ny + qq}

    def at_rep(zz, ll, cc):
        return {"replica": zz * 4 + ll * 2 + cc}

    x_peer = [at_fsdp(lax.rem(x + d, nx), q) for d in range(nx)]
    y_up = at_fsdp(x, lax.rem(q + 1, ny))
    y_down = at_fsdp(x, lax.rem(q + ny - 1, ny))
    z_of = [lax.rem(z + d, nz) for d in range(nz)]
    z_peer = [[at_rep(zz, yl, core), at_rep(zz, 1 - yl, core)] for zz in z_of]
    core_peer = at_rep(z, yl, 1 - core)
    lo_peer = z_peer[0][1]

    loads = []
    for k, (src, dst) in enumerate(
        [
            (cots, cot_own),
            (params.at[0], par),
            (first.at[0], mom1),
            (second.at[0], mom2),
            (anchor, anc.at[yl]),
            (outer_momentum, outer.at[yl]),
            (step, step_v),
        ]
    ):
        loads.append(pltpu.make_async_copy(src, dst, in_sem.at[k]))
        loads[-1].start()

    barrier = pltpu.get_barrier_semaphore()
    peers = x_peer[1:] + [y_up, y_down, core_peer] + [p for d in range(nz) for p in z_peer[d]][1:]
    for peer in peers:
        pl.semaphore_signal(
            barrier, inc=1, device_id=peer, device_id_type=pl.DeviceIdType.MESH
        )

    def owner_cols(xx, o):
        return pl.multiple_of((xx * ny + lax.rem(q + o, ny)) * width, width)

    own_feats = []
    for o in range(ny):
        own_feats.append(
            pltpu.make_async_copy(
                feats.at[:, pl.ds(owner_cols(x, o), width)],
                fbuf.at[o, 0],
                feat_sem.at[o],
            )
        )
        own_feats[-1].start()

    sent = []

    def send(src, dst, ssem, rsem, peer):
        copy = pltpu.make_async_remote_copy(
            src_ref=src,
            dst_ref=dst,
            send_sem=ssem,
            recv_sem=rsem,
            device_id=peer,
            device_id_type=pl.DeviceIdType.MESH,
        )
        copy.start()
        sent.append(copy)
        return copy

    loads[0].wait()
    turned = cot_own[...].astype(F32).T.reshape(4 * nz, 2, SUB, tokens)
    for u in (0, 1):
        cot_t[u * part : (u + 1) * part] = turned[:, u].reshape(part, tokens).astype(BF16)

    pl.semaphore_wait(barrier, len(peers))

    cot_copies = {}

    def cot_send(k):
        some = slice(k * quarter, (k + 1) * quarter)
        cot_copies[k] = [
            send(
                cot_t.at[some],
                cot_all.at[some, d * tokens : (d + 1) * tokens],
                cs.at[k, d - 1],
                cr.at[k, d - 1],
                x_peer[d],
            )
            for d in range(1, nx)
        ]

    x_copies = {}

    def x_send(c, o):
        x_copies[c, o] = [
            send(
                feats.at[:, pl.ds(owner_cols(lax.rem(x + d, nx), o) + c * cw, cw)],
                fbuf.at[o, d, :, c * cw : (c + 1) * cw],
                xs.at[c, o, d - 1],
                xr.at[c, o, d - 1],
                x_peer[d],
            )
            for d in range(1, nx)
        ]

    x_order = []
    for i, (c, lo, hi) in enumerate(y_units):
        ahead = y_units[i + 1 : i + 2] if i else y_units[:2]
        uses = [(a[0], 2) for a in ahead] + [(c, o) for o in (1, 3, 0)]
        for use in uses:
            if use not in x_order:
                x_order.append(use)
    x_done, cots_done = [0], [0]

    def x_upto(n):
        for use in x_order[x_done[0] : n]:
            x_send(*use)
        x_done[0] = max(x_done[0], n)

    def cots_upto(n):
        for k in range(cots_done[0], n):
            cot_send(k)
        cots_done[0] = max(cots_done[0], n)

    arrived = set()

    def block(c, o):
        x_upto(x_order.index((c, o)) + 1)
        if (c, o) not in arrived:
            arrived.add((c, o))
            if c == 0:
                own_feats[o].wait()
            for copy in x_copies[c, o]:
                copy.wait_recv()
        return fbuf[o, :, :, c * cw : (c + 1) * cw].reshape(nx * tokens, cw)

    def dot(lo, hi, cols):
        for k in range(lo // quarter, -(-hi // quarter)):
            for copy in cot_copies.pop(k, []):
                copy.wait_recv()
        return jnp.dot(cot_all[lo:hi], cols, preferred_element_type=F32)

    y_copies = {}

    def y_halves(i):
        c, lo, hi = y_units[i]
        mid = (lo + hi) // 2
        return c, (lo, mid), (mid, hi)

    def y_send(i, k, c, some, src, dst, peer):
        here = slice(*some)
        y_copies[i, k] = send(
            src.at[c, here], dst.at[c, here], ys.at[i, k], yr.at[i, k], peer
        )

    def far(i):
        c, a, b = y_halves(i)
        cols = block(c, 2)
        for k, some, peer in ((0, a, y_down), (1, b, y_up)):
            s1[c, slice(*some)] = dot(*some, cols).astype(BF16)
            y_send(i, k, c, some, s1, r1, peer)

    def near(i):
        c, a, b = y_halves(i)
        for k, o, direct, kept, peer in ((2, 1, a, b, y_up), (3, 3, b, a, y_down)):
            cols = block(c, o)
            sd[c, slice(*direct)] = dot(*direct, cols).astype(BF16)
            y_send(i, k, c, direct, sd, rd, peer)
            keep[c, slice(*kept)] = dot(*kept, cols)

    def relay(i):
        c, a, b = y_halves(i)
        for k, some, peer in ((0, a, y_down), (1, b, y_up)):
            here = slice(*some)
            y_copies[i, k].wait_recv()
            se[c, here] = (keep[c, here] + r1[c, here].astype(F32)).astype(BF16)
            y_send(i, 4 + k, c, some, se, r2, peer)

    def mine(c):
        cols = block(c, 0)
        for h in (0, 1):
            own[c, h * part : (h + 1) * part] = dot(h * part, (h + 1) * part, cols)

    rep_copies = {}

    def halves_of(j):
        c, us = r_units[j]
        return c, us, (slice(None) if len(us) == 2 else us[0])

    def adam(j):
        c, us, at = halves_of(j)
        if j == 0:
            for k in (1, 2, 3, 6):
                loads[k].wait()
        for i, (cc, lo, hi) in enumerate(y_units):
            if cc == c and any(lo < (u + 1) * part and u * part < hi for u in us):
                for k in (2, 3, 4, 5):
                    y_copies[i, k].wait_recv()
        t_value = jnp.full((1, cw), step_v[0].astype(F32), F32)
        rate = peak_rate * jnp.minimum(1.0, t_value / warm_steps)
        inv_one = 1.0 / (1.0 - jnp.exp(t_value * math.log(beta_one)))
        inv_two = 1.0 / (1.0 - jnp.exp(t_value * math.log(beta_two)))
        cols = slice(c * cw, (c + 1) * cw)

        def body(k, carry):
            here = pl.ds(pl.multiple_of(k * slab, slab), slab)
            for u in us:
                def rows_of(ref):
                    strip = ref[here, cols].astype(F32).reshape(4, 2, SUB, cw)
                    return strip[:, u].reshape(4 * SUB, cw)

                there = pl.ds(pl.multiple_of(u * part + k * (slab // 2), slab // 2), slab // 2)
                grad = own[c, there] + rd[c, there].astype(F32) + r2[c, there].astype(F32)
                weight = rows_of(par)
                m = beta_one * rows_of(mom1) + (1.0 - beta_one) * grad
                v = beta_two * rows_of(mom2) + (1.0 - beta_two) * grad * grad
                update = (m * inv_one) / (jnp.sqrt(v * inv_two) + 1e-08)
                new = weight - rate * (update + decay * weight)
                new = new.reshape(2, 2, SUB, cw)
                loc[c, 0, k, u] = new[:, 0]
                loc[c, 1, k, u] = new[:, 1]
            return carry

        lax.fori_loop(0, nz, body, 0)
        rep_copies[j, "core"] = send(
            loc.at[c, 1 - core, :, at], rcore.at[c, :, at], ks.at[j, 0], kr.at[j, 0], core_peer
        )

    z_first = [0]
    for flag in straight:
        z_first.append(z_first[-1] + (4 if flag else 2) * nz)

    def z_send(j, stage, d, e, src, dst):
        at = z_first[j] + ((stage * nz + d) * 2 + e if straight[j] else stage * nz + d)
        return send(src, dst, zs.at[at], zr.at[at], z_peer[d][e])

    def z_reduce(j):
        c, us, at = halves_of(j)
        rep_copies[j, "core"].wait_recv()
        copies = []
        for d in sorted(range(nz), key=lambda d: -min(d, nz - d)):
            zz = z_of[d]
            ssum[c, zz, at] = loc[c, core, zz, at] + rcore[c, zz, at]
            for e in (0, 1) if straight[j] else (0,):
                if d or e:
                    lo = (1 - yl if e else yl) if straight[j] else slice(None)
                    to = e if straight[j] else slice(None)
                    copies.append(
                        z_send(j, 0, d, e, ssum.at[c, zz, at, lo], rz.at[c, d, at, to])
                    )
        rep_copies[j, "z"] = copies

    def lo_reduce(j):
        c, us, at = halves_of(j)
        for copy in rep_copies[j, "z"]:
            copy.wait_recv()
        if straight[j]:
            total = ssum[c, z, at, yl] + rz[c, 0, at, 1]
            for d in range(1, nz):
                total = total + (rz[c, d, at, 0] + rz[c, d, at, 1])
            tot[c, at, 0] = total
        else:
            total = ssum[c, z, at]
            for d in range(1, nz):
                total = total + rz[c, d, at]
            tot[c, at] = total
            rep_copies[j, "lo"] = send(tot.at[c, at], ry.at[c, at], ls.at[j], lr.at[j], lo_peer)

    def outer_step(j):
        c, us, at = halves_of(j)
        cols = slice(c * cw, (c + 1) * cw)
        if not straight[j]:
            rep_copies[j, "lo"].wait_recv()
        for u in us:
            some = slice(u * SUB, (u + 1) * SUB)
            if straight[j]:
                total, who = tot[c, u, 0], yl
            else:
                total, who = tot[c, u] + ry[c, u], slice(None)
            old = anc[who, some, cols]
            delta = old - total * (1.0 / (4 * nz))
            momentum = outer_mu * outer[who, some, cols] + delta
            nxt[c, core, z, u, who] = old - outer_rate * (delta + outer_mu * momentum)
            momn[who, some, cols] = momentum
        piece = nxt.at[c, core, z, at, yl] if straight[j] else nxt.at[c, core, z, at]
        rep_copies[j, "z2"] = [
            z_send(j, 1, d, e, piece, piece)
            for d in sorted(range(nz), key=lambda d: -min(d, nz - d))
            for e in ((0, 1) if straight[j] else (0,))
            if d or e
        ]

    def core_gather(j):
        c, us, at = halves_of(j)
        for copy in rep_copies[j, "z2"]:
            copy.wait_recv()
        piece = nxt.at[c, core, :, at]
        rep_copies[j, "core2"] = send(piece, piece, ks.at[j, 1], kr.at[j, 1], core_peer)

    out_copies = []

    def merge(j):
        c, us, at = halves_of(j)
        rep_copies[j, "core2"].wait_recv()

        def body(k, carry):
            for u in us:
                for jc in (0, 1):
                    both = mix * loc[c, jc, k, u] + (1.0 - mix) * nxt[c, jc, k, u]
                    for e in (0, 1):
                        there = k * slab + ((2 * e + jc) * 2 + u) * SUB
                        mout[c, pl.ds(pl.multiple_of(there, SUB), SUB)] = both[e]
            return carry

        lax.fori_loop(0, nz, body, 0)
        if 1 in us:
            copy = pltpu.make_async_copy(
                mout.at[c], merged_out.at[0, :, c * cw : (c + 1) * cw], os.at[c]
            )
            copy.start()
            out_copies.append(copy)

    outer_copies = []

    def outer_send():
        for k, (src, dst) in enumerate([(anchor, anc), (outer_momentum, outer)]):
            outer_copies.append(send(src, dst.at[yl], os_.at[0, k], os_.at[1, k], lo_peer))

    def outer_wait():
        for copy in loads[4:6]:
            copy.wait()
        for copy in outer_copies:
            copy.wait_recv()

    cots_upto(1), x_upto(1), cots_upto(2)
    cot_all[:, 0:tokens] = cot_t[...]
    cots_upto(4), x_upto(4), far(0)
    x_upto(7), far(1)
    x_upto(9), near(0)
    x_upto(11), relay(0)
    near(1)
    relay(1)
    outer_send(), mine(0)
    x_upto(12), far(2)
    x_upto(13), far(3)
    near(2)
    x_upto(15), near(3)
    adam(0)
    x_upto(16), mine(1)
    relay(2)
    far(4)
    far(5)
    z_reduce(0)
    relay(3)
    near(4)
    near(5)
    mine(2)
    lo_reduce(0)
    far(6)
    relay(4)
    relay(5)
    adam(1)
    far(7)
    near(6)
    z_reduce(1)
    outer_wait(), outer_step(0)
    near(7)
    mine(3)
    relay(6)
    adam(2)
    lo_reduce(1)
    relay(7)
    z_reduce(2)
    core_gather(0)
    merge(0)
    adam(3)
    outer_step(1)
    adam(4)
    lo_reduce(2)
    z_reduce(3)
    z_reduce(4)
    outer_step(2)
    core_gather(1)
    lo_reduce(3)
    merge(1)
    outer_step(3)
    lo_reduce(4)
    outer_step(4)
    core_gather(2)
    core_gather(3)
    merge(2)
    core_gather(4)
    merge(3)
    merge(4)
    momentum_copy = pltpu.make_async_copy(momn.at[yl], momentum_out, os.at[nc])
    momentum_copy.start()
    for copy in sent:
        copy.wait_send()
    for copy in out_copies:
        copy.wait()
    momentum_copy.wait()


def per_device(features, cotangents, params, first, second, anchor, outer_momentum, step, *, nx, nz, nc):
    tokens = features.shape[0]
    rows, width = params.shape[1:]
    cw = width // nc
    piece = anchor.shape[0]
    part = rows // 2
    y_units = [(c, h * part, (h + 1) * part) for c in range(nc) for h in (0, 1)]
    r_units = [(c, (0, 1)) for c in range(nc - 1)] + [(nc - 1, (0,)), (nc - 1, (1,))]
    straight = [len(us) == 1 for c, us in r_units]
    ny_, nr_ = len(y_units), len(r_units)
    nz_ = sum(4 * nz if flag else 2 * nz for flag in straight)
    hbm = pl.BlockSpec(memory_space=pl.ANY)
    dma = pltpu.SemaphoreType.DMA
    operands = [
        pltpu.with_memory_space_constraint(a, pltpu.HBM)
        for a in (features, cotangents, params, first, second, anchor, outer_momentum)
    ]
    return pl.pallas_call(
        functools.partial(kernel, nx, nz, nc, y_units, r_units, straight),
        out_shape=(
            jax.ShapeDtypeStruct((1, rows, width), F32),
            jax.ShapeDtypeStruct((piece, width), F32),
        ),
        in_specs=[hbm] * 8,
        out_specs=(hbm, hbm),
        scratch_shapes=[
            pltpu.VMEM((tokens, rows), BF16),
            pltpu.VMEM((rows, tokens), BF16),
            pltpu.VMEM((rows, nx * tokens), BF16),
            pltpu.VMEM((NY, nx, tokens, width), BF16),
            pltpu.VMEM((rows, width), BF16),
            pltpu.VMEM((rows, width), BF16),
            pltpu.VMEM((rows, width), BF16),
            pltpu.VMEM((2, piece, width), F32),
            pltpu.VMEM((2, piece, width), F32),
            pltpu.VMEM((nc, rows, cw), F32),
            pltpu.VMEM((nc, rows, cw), F32),
            pltpu.VMEM((nc, rows, cw), BF16),
            pltpu.VMEM((nc, rows, cw), BF16),
            pltpu.VMEM((nc, rows, cw), BF16),
            pltpu.VMEM((nc, rows, cw), BF16),
            pltpu.VMEM((nc, rows, cw), BF16),
            pltpu.VMEM((nc, rows, cw), BF16),
            pltpu.VMEM((nc, 2, nz, 2, 2, SUB, cw), F32),
            pltpu.VMEM((nc, nz, 2, 2, SUB, cw), F32),
            pltpu.VMEM((nc, nz, 2, 2, SUB, cw), F32),
            pltpu.VMEM((nc, nz, 2, 2, SUB, cw), F32),
            pltpu.VMEM((nc, 2, 2, SUB, cw), F32),
            pltpu.VMEM((nc, 2, 2, SUB, cw), F32),
            pltpu.VMEM((nc, 2, nz, 2, 2, SUB, cw), F32),
            pltpu.VMEM((nc, rows, cw), F32),
            pltpu.VMEM((2, piece, width), F32),
            pltpu.SMEM((1,), jnp.int32),
            dma((7,)), dma((NY,)),
            dma((4, nx - 1)), dma((4, nx - 1)),
            dma((nc, NY, nx - 1)), dma((nc, NY, nx - 1)),
            dma((ny_, 6)), dma((ny_, 6)),
            dma((nr_, 2)), dma((nr_, 2)),
            dma((2, 2)),
            dma((nz_,)), dma((nz_,)),
            dma((nr_,)), dma((nr_,)),
            dma((nc + 1,)),
        ],
        compiler_params=pltpu.CompilerParams(
            collective_id=0, has_side_effects=True, vmem_limit_bytes=48 * 1024 * 1024
        ),
    )(*operands, step)


def build(mesh, nx, nz, nc):
    in_specs = (
        P(("replica", "fsdp"), None),
        P(("replica", "fsdp"), None),
        P("replica", None, "fsdp"),
        P("replica", None, "fsdp"),
        P("replica", None, "fsdp"),
        P("replica", "fsdp"),
        P("replica", "fsdp"),
        P(),
    )
    out_specs = (P("replica", None, "fsdp"), P("replica", "fsdp"))
    return jax.shard_map(
        functools.partial(per_device, nx=nx, nz=nz, nc=nc),
        mesh=mesh, in_specs=in_specs, out_specs=out_specs, check_vma=False,
    )


def solution(mesh):
    return build(mesh, NX, NZ, CHUNKS)
```

time: 90.9 us -> 86.5 us (0.952)
  Pallas kernels: 87.8 us -> 83.4 us
    pallas_call x1, Pallas kernels: 87.8 us -> 83.4 us  [per_device(): pl.pallas_call(functools.partial(kernel, nx, nz, nc, y_units, r_units, st...]
where the time goes in v3:
time: 86.5 us; the launch traced here: 86.3 us
  Pallas kernels  83.4 us (96%)
  local copies, waits for them, and re-layouts  1.59 us (2%)
  between operations  1.29 us (1%)
    pallas_call x1, Pallas kernels, per_device(): pl.pallas_call(functools.partial(kernel, nx, nz, nc, y_units, r_units, st...  83.4 us

profile of v3, /device:TPU:1, one launch (start us, length us, event | category | flops | bytes accessed | tf_op | source)
XLA Modules:
  0.0 86.3 jit_solution(2051626062199817099)
XLA Ops:
  1.3 83.4 %shard_map.95 = (f32[1,512,512]{2,1,0:T(8,128)S(1)}, f32[16,512]{1,0:T(8,128)S(1)}) custom-call(bf16[128,8192]{1,0:T(8,128)(2,1)} %feats.1, bf16[128,512]{1,0:T(8,128)(2,1)} %cots.1, bf16[1,512,512]{2,1,0:T(8,128)(2,1)} %params.1, bf16[1,512,512]{2,1,0:T(8,128)(2,1)} %first.1, bf16[1,512,512]{2,1,0:T(8,128)(2,1)} %second.1, f32[16,512]{1,0:T(8,128)} %anchor.1, ...), custom_call_target="tpu_custom_call" | custom-call | tf_op jit(solution)/shard_map/pallas_call | solution.py:466
  84.7 1.0 %copy.13 = f32[1,512,512]{2,1,0:T(8,128)} copy(f32[1,512,512]{2,1,0:T(8,128)S(1)} %get-tuple-element.4) | data formatting | bytes 2097152
  85.7 0.6 copy.14

commit v4 on v3

--- a/solution.py
+++ b/solution.py
@@ -29,8 +29,8 @@
     merged_out, momentum_out,
     cot_own, cot_t, cot_all, fbuf, par, mom1, mom2, anc, outer,
     own, keep, s1, sd, se, r1, rd, r2,
-    loc, rcore, ssum, rz, tot, ry, nxt, mout, momn,
-    step_v, in_sem, feat_sem, cs, cr, xs, xr, ys, yr, ks, kr, os_, zs, zr, ls, lr, os,
+    loc, rcore, ssum, rz, tot, ry, nxt,
+    step_v, in_sem, feat_sem, cs, cr, xs, xr, ys, yr, ks, kr, os_, zs, zr, ls, lr,
 ):
     ny = NY
     rows, width = par.shape
@@ -150,7 +150,7 @@
 
     x_order = []
     for i, (c, lo, hi) in enumerate(y_units):
-        ahead = y_units[i + 1 : i + 2] if i else y_units[:2]
+        ahead = y_units[: i + 2]
         uses = [(a[0], 2) for a in ahead] + [(c, o) for o in (1, 3, 0)]
         for use in uses:
             if use not in x_order:
@@ -326,7 +326,7 @@
             delta = old - total * (1.0 / (4 * nz))
             momentum = outer_mu * outer[who, some, cols] + delta
             nxt[c, core, z, u, who] = old - outer_rate * (delta + outer_mu * momentum)
-            momn[who, some, cols] = momentum
+            momentum_out[some, cols] = momentum if straight[j] else jnp.where(yl == 0, momentum[0], momentum[1])
         piece = nxt.at[c, core, z, at, yl] if straight[j] else nxt.at[c, core, z, at]
         rep_copies[j, "z2"] = [
             z_send(j, 1, d, e, piece, piece)
@@ -342,11 +342,10 @@
         piece = nxt.at[c, core, :, at]
         rep_copies[j, "core2"] = send(piece, piece, ks.at[j, 1], kr.at[j, 1], core_peer)
 
-    out_copies = []
-
     def merge(j):
         c, us, at = halves_of(j)
         rep_copies[j, "core2"].wait_recv()
+        cols = slice(c * cw, (c + 1) * cw)
 
         def body(k, carry):
             for u in us:
@@ -354,16 +353,10 @@
                     both = mix * loc[c, jc, k, u] + (1.0 - mix) * nxt[c, jc, k, u]
                     for e in (0, 1):
                         there = k * slab + ((2 * e + jc) * 2 + u) * SUB
-                        mout[c, pl.ds(pl.multiple_of(there, SUB), SUB)] = both[e]
+                        merged_out[0, pl.ds(pl.multiple_of(there, SUB), SUB), cols] = both[e]
             return carry
 
         lax.fori_loop(0, nz, body, 0)
-        if 1 in us:
-            copy = pltpu.make_async_copy(
-                mout.at[c], merged_out.at[0, :, c * cw : (c + 1) * cw], os.at[c]
-            )
-            copy.start()
-            out_copies.append(copy)
 
     outer_copies = []
 
@@ -379,56 +372,50 @@
 
     cots_upto(1), x_upto(1), cots_upto(2)
     cot_all[:, 0:tokens] = cot_t[...]
-    cots_upto(4), x_upto(4), far(0)
-    x_upto(7), far(1)
-    x_upto(9), near(0)
-    x_upto(11), relay(0)
-    near(1)
-    relay(1)
+    x_upto(3), far(0)
+    cots_upto(4), x_upto(4), near(0)
+    x_upto(6), relay(0)
+    far(1)
+    x_upto(8), near(1)
     outer_send(), mine(0)
-    x_upto(12), far(2)
-    x_upto(13), far(3)
-    near(2)
-    x_upto(15), near(3)
-    adam(0)
-    x_upto(16), mine(1)
+    x_upto(9), far(2)
+    x_upto(10), relay(1)
+    far(3)
+    x_upto(11), near(2)
+    x_upto(13), mine(1)
+    x_upto(14), adam(0)
     relay(2)
+    x_upto(15), z_reduce(0)
     far(4)
-    far(5)
-    z_reduce(0)
-    relay(3)
-    near(4)
-    near(5)
+    x_upto(16), near(3)
     mine(2)
     lo_reduce(0)
-    far(6)
+    adam(1)
+    relay(3)
+    z_reduce(1)
+    far(5)
+    outer_wait(), outer_step(0)
+    near(4)
     relay(4)
-    relay(5)
-    adam(1)
-    far(7)
-    near(6)
-    z_reduce(1)
-    outer_wait(), outer_step(0)
-    near(7)
-    mine(3)
-    relay(6)
     adam(2)
     lo_reduce(1)
-    relay(7)
+    near(5)
+    mine(3)
     z_reduce(2)
+    relay(5)
     core_gather(0)
-    merge(0)
     adam(3)
     outer_step(1)
+    merge(0)
+    z_reduce(3)
     adam(4)
     lo_reduce(2)
-    z_reduce(3)
     z_reduce(4)
     outer_step(2)
     core_gather(1)
     lo_reduce(3)
+    outer_step(3)
     merge(1)
-    outer_step(3)
     lo_reduce(4)
     outer_step(4)
     core_gather(2)
@@ -437,13 +424,8 @@
     core_gather(4)
     merge(3)
     merge(4)
-    momentum_copy = pltpu.make_async_copy(momn.at[yl], momentum_out, os.at[nc])
-    momentum_copy.start()
     for copy in sent:
         copy.wait_send()
-    for copy in out_copies:
-        copy.wait()
-    momentum_copy.wait()
 
 
 def per_device(features, cotangents, params, first, second, anchor, outer_momentum, step, *, nx, nz, nc):
@@ -452,7 +434,9 @@
     cw = width // nc
     piece = anchor.shape[0]
     part = rows // 2
-    y_units = [(c, h * part, (h + 1) * part) for c in range(nc) for h in (0, 1)]
+    y_units = [(0, 0, part), (0, part, rows)]
+    y_units += [(c, 0, rows) for c in range(1, nc - 1)]
+    y_units += [(nc - 1, 0, part), (nc - 1, part, rows)]
     r_units = [(c, (0, 1)) for c in range(nc - 1)] + [(nc - 1, (0,)), (nc - 1, (1,))]
     straight = [len(us) == 1 for c, us in r_units]
     ny_, nr_ = len(y_units), len(r_units)
@@ -470,7 +454,7 @@
             jax.ShapeDtypeStruct((piece, width), F32),
         ),
         in_specs=[hbm] * 8,
-        out_specs=(hbm, hbm),
+        out_specs=(pl.BlockSpec(memory_space=pltpu.VMEM),) * 2,
         scratch_shapes=[
             pltpu.VMEM((tokens, rows), BF16),
             pltpu.VMEM((rows, tokens), BF16),
@@ -496,8 +480,6 @@
             pltpu.VMEM((nc, 2, 2, SUB, cw), F32),
             pltpu.VMEM((nc, 2, 2, SUB, cw), F32),
             pltpu.VMEM((nc, 2, nz, 2, 2, SUB, cw), F32),
-            pltpu.VMEM((nc, rows, cw), F32),
-            pltpu.VMEM((2, piece, width), F32),
             pltpu.SMEM((1,), jnp.int32),
             dma((7,)), dma((NY,)),
             dma((4, nx - 1)), dma((4, nx - 1)),
@@ -507,7 +489,6 @@
             dma((2, 2)),
             dma((nz_,)), dma((nz_,)),
             dma((nr_,)), dma((nr_,)),
-            dma((nc + 1,)),
         ],
         compiler_params=pltpu.CompilerParams(
             collective_id=0, has_side_effects=True, vmem_limit_bytes=48 * 1024 * 1024

time: 86.5 us -> 84.5 us (0.977)
  Pallas kernels: 83.4 us -> 81.4 us
    pallas_call x1, Pallas kernels: 83.4 us -> 81.4 us  [per_device(): pl.pallas_call(functools.partial(kernel, nx, nz, nc, y_units, r_units, st...]
where the time goes in v4:
time: 84.5 us; the launch traced here: 84.3 us
  Pallas kernels  81.4 us (96%)
  local copies, waits for them, and re-layouts  1.59 us (2%)
  between operations  1.29 us (2%)
    pallas_call x1, Pallas kernels, per_device(): pl.pallas_call(functools.partial(kernel, nx, nz, nc, y_units, r_units, st...  81.4 us

profile of v4, /device:TPU:1, one launch (start us, length us, event | category | flops | bytes accessed | tf_op | source)
XLA Modules:
  0.0 84.3 jit_solution(1166204787903186268)
XLA Ops:
  1.3 81.4 %shard_map.95 = (f32[1,512,512]{2,1,0:T(8,128)S(1)}, f32[16,512]{1,0:T(8,128)S(1)}) custom-call(bf16[128,8192]{1,0:T(8,128)(2,1)} %feats.1, bf16[128,512]{1,0:T(8,128)(2,1)} %cots.1, bf16[1,512,512]{2,1,0:T(8,128)(2,1)} %params.1, bf16[1,512,512]{2,1,0:T(8,128)(2,1)} %first.1, bf16[1,512,512]{2,1,0:T(8,128)(2,1)} %second.1, f32[16,512]{1,0:T(8,128)} %anchor.1, ...), custom_call_target="tpu_custom_call" | custom-call | tf_op jit(solution)/shard_map/pallas_call | solution.py:450
  82.7 1.0 %copy.13 = f32[1,512,512]{2,1,0:T(8,128)} copy(f32[1,512,512]{2,1,0:T(8,128)S(1)} %get-tuple-element.4) | data formatting | bytes 2097152
  83.7 0.6 copy.14

commit v5 on v4

--- a/solution.py
+++ b/solution.py
@@ -24,7 +24,7 @@
 
 
 def kernel(
-    nx, nz, nc, y_units, r_units, straight,
+    nx, nz, nc, y_units, r_units, straight, split,
     feats, cots, params, first, second, anchor, outer_momentum, step,
     merged_out, momentum_out,
     cot_own, cot_t, cot_all, fbuf, par, mom1, mom2, anc, outer,
@@ -74,7 +74,8 @@
         ]
     ):
         loads.append(pltpu.make_async_copy(src, dst, in_sem.at[k]))
-        loads[-1].start()
+        if k == 0:
+            loads[-1].start()
 
     barrier = pltpu.get_barrier_semaphore()
     peers = x_peer[1:] + [y_up, y_down, core_peer] + [p for d in range(nz) for p in z_peer[d]][1:]
@@ -309,7 +310,7 @@
             for d in range(1, nz):
                 total = total + rz[c, d, at]
             tot[c, at] = total
-            rep_copies[j, "lo"] = send(tot.at[c, at], ry.at[c, at], ls.at[j], lr.at[j], lo_peer)
+            rep_copies[j, "lo"] = send(tot.at[c, at], ry.at[c, at], ls.at[0, j], lr.at[0, j], lo_peer)
 
     def outer_step(j):
         c, us, at = halves_of(j)
@@ -320,14 +321,16 @@
             some = slice(u * SUB, (u + 1) * SUB)
             if straight[j]:
                 total, who = tot[c, u, 0], yl
+            elif split[j]:
+                total, who = tot[c, u, yl] + ry[c, u, yl], yl
             else:
                 total, who = tot[c, u] + ry[c, u], slice(None)
             old = anc[who, some, cols]
             delta = old - total * (1.0 / (4 * nz))
             momentum = outer_mu * outer[who, some, cols] + delta
             nxt[c, core, z, u, who] = old - outer_rate * (delta + outer_mu * momentum)
-            momentum_out[some, cols] = momentum if straight[j] else jnp.where(yl == 0, momentum[0], momentum[1])
-        piece = nxt.at[c, core, z, at, yl] if straight[j] else nxt.at[c, core, z, at]
+            momentum_out[some, cols] = momentum if straight[j] or split[j] else jnp.where(yl == 0, momentum[0], momentum[1])
+        piece = nxt.at[c, core, z, at, yl] if straight[j] or split[j] else nxt.at[c, core, z, at]
         rep_copies[j, "z2"] = [
             z_send(j, 1, d, e, piece, piece)
             for d in sorted(range(nz), key=lambda d: -min(d, nz - d))
@@ -335,9 +338,16 @@
             if d or e
         ]
 
+    def lo_gather(j):
+        c, us, at = halves_of(j)
+        for copy in rep_copies[j, "z2"]:
+            copy.wait_recv()
+        piece = nxt.at[c, core, :, at, yl]
+        rep_copies[j, "lo2"] = send(piece, piece, ls.at[1, j], lr.at[1, j], lo_peer)
+
     def core_gather(j):
         c, us, at = halves_of(j)
-        for copy in rep_copies[j, "z2"]:
+        for copy in [rep_copies[j, "lo2"]] if split[j] else rep_copies[j, "z2"]:
             copy.wait_recv()
         piece = nxt.at[c, core, :, at]
         rep_copies[j, "core2"] = send(piece, piece, ks.at[j, 1], kr.at[j, 1], core_peer)
@@ -373,6 +383,8 @@
     cots_upto(1), x_upto(1), cots_upto(2)
     cot_all[:, 0:tokens] = cot_t[...]
     x_upto(3), far(0)
+    for copy in loads[1:]:
+        copy.start()
     cots_upto(4), x_upto(4), near(0)
     x_upto(6), relay(0)
     far(1)
@@ -399,9 +411,9 @@
     relay(4)
     adam(2)
     lo_reduce(1)
+    z_reduce(2)
     near(5)
     mine(3)
-    z_reduce(2)
     relay(5)
     core_gather(0)
     adam(3)
@@ -412,17 +424,19 @@
     lo_reduce(2)
     z_reduce(4)
     outer_step(2)
-    core_gather(1)
+    lo_gather(1)
     lo_reduce(3)
     outer_step(3)
-    merge(1)
+    core_gather(1)
     lo_reduce(4)
     outer_step(4)
+    lo_gather(2)
+    merge(1)
+    core_gather(3)
     core_gather(2)
-    core_gather(3)
-    merge(2)
     core_gather(4)
     merge(3)
+    merge(2)
     merge(4)
     for copy in sent:
         copy.wait_send()
@@ -439,6 +453,7 @@
     y_units += [(nc - 1, 0, part), (nc - 1, part, rows)]
     r_units = [(c, (0, 1)) for c in range(nc - 1)] + [(nc - 1, (0,)), (nc - 1, (1,))]
     straight = [len(us) == 1 for c, us in r_units]
+    split = [0 < c < nc - 1 for c, us in r_units]
     ny_, nr_ = len(y_units), len(r_units)
     nz_ = sum(4 * nz if flag else 2 * nz for flag in straight)
     hbm = pl.BlockSpec(memory_space=pl.ANY)
@@ -448,7 +463,7 @@
         for a in (features, cotangents, params, first, second, anchor, outer_momentum)
     ]
     return pl.pallas_call(
-        functools.partial(kernel, nx, nz, nc, y_units, r_units, straight),
+        functools.partial(kernel, nx, nz, nc, y_units, r_units, straight, split),
         out_shape=(
             jax.ShapeDtypeStruct((1, rows, width), F32),
             jax.ShapeDtypeStruct((piece, width), F32),
@@ -488,7 +503,7 @@
             dma((nr_, 2)), dma((nr_, 2)),
             dma((2, 2)),
             dma((nz_,)), dma((nz_,)),
-            dma((nr_,)), dma((nr_,)),
+            dma((2, nr_)), dma((2, nr_)),
         ],
         compiler_params=pltpu.CompilerParams(
             collective_id=0, has_side_effects=True, vmem_limit_bytes=48 * 1024 * 1024

time: 84.5 us -> 84.4 us (level)
  no operation moved by 1% of the time
where the time goes in v5:
time: 84.4 us; the launch traced here: 84.3 us
  Pallas kernels  81.4 us (96%)
  local copies, waits for them, and re-layouts  1.59 us (2%)
  between operations  1.29 us (2%)
    pallas_call x1, Pallas kernels, per_device(): pl.pallas_call(functools.partial(kernel, nx, nz, nc, y_units, r_units, st...  81.4 us

profile of v5, /device:TPU:1, one launch (start us, length us, event | category | flops | bytes accessed | tf_op | source)
XLA Modules:
  0.0 84.3 jit_solution(2438454688501032967)
XLA Ops:
  1.3 81.4 %shard_map.95 = (f32[1,512,512]{2,1,0:T(8,128)S(1)}, f32[16,512]{1,0:T(8,128)S(1)}) custom-call(bf16[128,8192]{1,0:T(8,128)(2,1)} %feats.1, bf16[128,512]{1,0:T(8,128)(2,1)} %cots.1, bf16[1,512,512]{2,1,0:T(8,128)(2,1)} %params.1, bf16[1,512,512]{2,1,0:T(8,128)(2,1)} %first.1, bf16[1,512,512]{2,1,0:T(8,128)(2,1)} %second.1, f32[16,512]{1,0:T(8,128)} %anchor.1, ...), custom_call_target="tpu_custom_call" | custom-call | tf_op jit(solution)/shard_map/pallas_call | solution.py:465
  82.7 1.0 %copy.13 = f32[1,512,512]{2,1,0:T(8,128)} copy(f32[1,512,512]{2,1,0:T(8,128)S(1)} %get-tuple-element.4) | data formatting | bytes 2097152
  83.7 0.6 copy.14
